TPU v7x, 256 devices: a whole 4x4x8 slice. The times are simulated.
256 devices in a mesh: head: 16 (over x, y), key: 8 (over z), row: 2 (over core).
Axes of the slice: x: 4, y: 4, z: 8, core: 2. Of those that a mesh axis runs over, the one named last changes fastest.
Arguments:
- mla_query: bfloat16 [256, 128, 576], P('row', 'head'), may hold values from -48 to 48
- mla_cache: bfloat16 [16, 2048, 576], P(None, 'key'), may hold values from -6 to 6
- index_query: bfloat16 [256, 64, 128], P('row'), may hold values from -24 to 24
- index_keys: bfloat16 [32768, 128], P(('head', 'key')), may hold values from -6 to 6
- index_weight: float32 [256, 64], P('row'), may hold values from -0.75 to 0.75
Outputs:
- query_grad: float32 [256, 64, 128], P('row', 'head')
- key_grad: float32 [32768, 128], P(('head', 'key', 'row'))
- weight_grad: float32 [256, 64], P('row')
All inputs are finite; a program needn't handle non-finite values.
Results may differ from a plain program's by a relative error of at most 0.0029.
Values sent between devices are 32-bit elements; how exact they have to be, the bound alone decides.
No kernel may reach another device: no remote copies, remote signals or barrier semaphores. Data moves between devices by JAX's collectives and lax.ppermute only.
A program may use at most 128 MiB of HBM per device.

v0:
```python
import math
import jax
import jax.numpy as jnp
from jax import lax
from jax.sharding import PartitionSpec as P

MH = 128


def shards(mla_query, mla_cache, index_query, index_keys, index_weight):
    key_count = lax.axis_size("key")
    head_count = lax.axis_size("head")
    block_count = mla_cache.shape[0]
    local_keys = mla_cache.shape[1]
    row_local = mla_query.shape[0]
    cache_rows = mla_cache.reshape(block_count * local_keys, mla_cache.shape[2])
    scores = jnp.einsum(
        "thd,sd->ths", mla_query, cache_rows, preferred_element_type=jnp.float32
    ) * (1.0 / math.sqrt(192.0))
    top_score = lax.pmax(jnp.max(scores, axis=2), "key")
    exp_terms = jnp.exp(scores - top_score[:, :, None])
    sum_terms = lax.psum(jnp.sum(exp_terms, axis=2), "key")
    head_scale = 1.0 / sum_terms
    partial_value = jnp.sum(exp_terms * head_scale[:, :, None], axis=1) / MH
    spread = partial_value.reshape(row_local, block_count, local_keys)
    summed_all = lax.psum(spread, "head")
    target = lax.dynamic_slice_in_dim(summed_all, lax.axis_index("head"), 1, 1).reshape(
        row_local, local_keys
    )
    root_width = math.sqrt(index_keys.shape[1])
    products = jnp.einsum(
        "thd,sd->ths", index_query, index_keys, preferred_element_type=jnp.float32
    )
    active = jnp.maximum(products, 0.0)
    logits = jnp.sum(active * index_weight[:, :, None], axis=1) / root_width
    top_logit = lax.pmax(jnp.max(logits, axis=1), ("head", "key"))
    exp_logit = jnp.exp(logits - top_logit[:, None])
    logit_sum = lax.psum(jnp.sum(exp_logit, axis=1), ("head", "key"))
    soft_probs = exp_logit / logit_sum[:, None]
    key_total = index_keys.shape[0] * head_count * key_count
    dlogits = key_total * (soft_probs - target)
    weight_part = jnp.sum(active * dlogits[:, None, :], axis=2) / root_width
    slope_terms = (
        dlogits[:, None, :]
        * index_weight[:, :, None]
        * jnp.where(products > 0.0, 1.0, 0.0)
        / root_width
    ).astype(jnp.bfloat16)
    query_part = jnp.einsum(
        "ths,sd->thd", slope_terms, index_keys, preferred_element_type=jnp.float32
    )
    keys_part = jnp.einsum(
        "ths,thd->sd", slope_terms, index_query, preferred_element_type=jnp.float32
    )
    key_grad = lax.psum_scatter(keys_part, "row", scatter_dimension=0, tiled=True)
    head_share = query_part.shape[1] // head_count
    query_full, weight_grad = lax.psum((query_part, weight_part), ("head", "key"))
    query_grad = lax.dynamic_slice_in_dim(
        query_full, lax.axis_index("head") * head_share, head_share, 1
    )
    return (query_grad, key_grad, weight_grad)


def solution(mesh):
    placed = (
        P("row", "head", None),
        P(None, "key", None),
        P("row", None, None),
        P(("head", "key"), None),
        P("row", None),
    )
    return jax.shard_map(
        shards,
        mesh=mesh,
        in_specs=placed,
        out_specs=(P("row", "head", None), P(("head", "key", "row"), None), P("row", None)),
        check_vma=False,
    )
```

profile of v0, /device:TPU:0, one launch (start us, length us, event | category | flops | bytes accessed | tf_op | source)
XLA Modules:
  0.0 1499.3 jit_solution(123140552502343702)
XLA Ops:
  7.2 0.0 copy-start
  7.2 0.0 all-reduce.3.cloned.1.call-start
  7.2 7.2 copy.19
  14.4 8.3 reshape.73
  22.7 0.0 copy-done
  22.7 12.6 multiply_reduce_fusion.1
  35.3 18.2 %pmax.15 = f32[128,8]{0,1:T(8,128)S(1)} all-reduce(f32[128,8]{0,1:T(8,128)S(1)} %get-tuple-element.12), channel_id=1, replica_groups=mesh['head'=16,'key'=8,'row'=2] {'key'}, use_global_device_ids=true, to_apply=%region_6.0 | all-reduce | flops 1024 | bytes 8192 | tf_op jit(solution)/shard_map/pmax | solution.py:20
  53.6 8.6 fusion
  62.2 14.2 psum.36
  76.4 8.0 multiply_reduce_fusion
  84.4 0.0 copy-start.2
  84.4 0.0 copy-start.3
  84.4 0.2 broadcast_multiply_fusion
  84.6 1.9 copy.20
  86.4 3.0 copy.21
  89.4 0.0 all-reduce.3.cloned.1.call-update
  89.4 0.2 all-reduce.5.cloned.1.call-start
  89.7 0.0 copy-done.2
  89.7 0.0 copy-done.3
  89.7 6.8 multiply_reduce_fusion.3
  96.4 0.1 multiply_reduce_fusion.4
  96.5 349.1 %pmax.14 = f32[128]{0:T(128)S(1)} all-reduce(f32[128]{0:T(128)S(1)} %multiply_reduce_fusion.4), channel_id=1, replica_groups=mesh['head'=16,'key'=8,'row'=2] {'head','key'}, use_global_device_ids=true, to_apply=%region_2.0 | all-reduce | flops 128 | bytes 1024 | tf_op jit(solution)/shard_map/pmax | solution.py:36
  445.7 0.2 exponential_reduce_fusion
  445.9 342.2 %psum.35 = f32[128]{0:T(128)S(1)} all-reduce(f32[128]{0:T(128)S(1)} %exponential_reduce_fusion), channel_id=1, replica_groups=mesh['head'=16,'key'=8,'row'=2] {'head','key'}, use_global_device_ids=true, to_apply=%region_4.0 | all-reduce | flops 128 | bytes 1024 | tf_op jit(solution)/shard_map/psum | solution.py:38
  788.0 0.0 all-reduce.3.cloned.1.call-done
  788.0 1.0 fusion.12
  789.1 5.7 fusion.13
  794.8 0.0 copy-start.1
  794.8 0.0 all-reduce.5.cloned.1.call-update
  794.8 0.0 reduce-scatter.2.cloned.1.call-start
  794.9 4.7 multiply_reduce_fusion.2
  799.6 0.0 copy-done.1
  799.6 7.0 fusion.5
  806.6 0.0 reduce-scatter.2.cloned.1.call-update
  806.6 684.3 %psum.39 = f32[128,64]{0,1:T(8,128)} all-reduce(f32[128,64]{0,1:T(8,128)S(1)} %broadcast_multiply_fusion.1), channel_id=1, replica_groups=mesh['head'=16,'key'=8,'row'=2] {'head','key'}, use_global_device_ids=true, to_apply=%region_14.15 | all-reduce | flops 8192 | bytes 65536 | tf_op jit(solution)/shard_map/psum | solution.py:57
  1490.9 0.0 all-reduce.5.cloned.1.call-done
  1490.9 1.0 constant_dynamic-slice_fusion
  1491.9 0.9 copy.24
  1492.8 0.0 reduce-scatter.2.cloned.1.call-done
  (2 shorter events, 0.0 us)
Async XLA Ops:
  7.2 15.6 %copy-start = (bf16[128,8,576]{0,2,1:T(8,128)(2,1)S(1)}, bf16[128,8,576]{0,2,1:T(8,128)(2,1)}, u32[]{:S(2)}) copy-start(bf16[128,8,576]{0,2,1:T(8,128)(2,1)} %param.5) | copy-start | bytes 3538948
  7.2 780.8 %all-reduce.3.cloned.1.call-start = ((), (), s32[]{:S(2)}) async-start(), calls=%async_computation.1 | async-start | bytes 4194304 | tf_op jit(solution)/shard_map/psum | solution.py:26
  84.4 5.3 copy-start.2
  84.4 5.3 copy-start.3
  89.4 1401.5 %all-reduce.5.cloned.1.call-start = ((), (), s32[]{:S(2)}) async-start(), calls=%async_computation.2 | async-start | bytes 8388608 | tf_op jit(solution)/shard_map/psum | solution.py:57
  794.8 4.8 copy-start.1
  794.8 697.9 %reduce-scatter.2.cloned.1.call-start = ((), (), s32[]{:S(2)}) async-start(), calls=%async_computation.3 | async-start | bytes 196608 | tf_op jit(solution)/shard_map/reduce_scatter | solution.py:55
Sparse Core Ops, SparseCore 0:
  89.5 99.6 all-reduce.2
  795.0 227.7 all-reduce.4
  1025.8 10.1 reduce-scatter.1
where the time goes:
time: 1500 us
  blocking collectives  1410 us (94%)
  matrix products  32.1 us (2%)
  other arithmetic  22.8 us (2%)
  local copies, waits for them, and re-layouts  22.2 us (1%)
    psum x1, blocking collectives, shards(): lax.psum((query_part, weight_part), ('head', 'key'))  684 us
    pmax x1, blocking collectives, shards(): top_logit = lax.pmax(jnp.max(logits, axis=1), ('head', 'key'))  349 us
    psum x1, blocking collectives, shards(): logit_sum = lax.psum(jnp.sum(exp_logit, axis=1), ('head', 'key'))  342 us
  transfers between devices with their start and end apart: 3, of which 0 were waited for; matrix products, arithmetic and copies ran while one was open for 1% of the time, Pallas kernels for 0%

commit v1 on v0

--- a/solution.py
+++ b/solution.py
@@ -35,7 +35,9 @@
     logits = jnp.sum(active * index_weight[:, :, None], axis=1) / root_width
     top_logit = lax.pmax(jnp.max(logits, axis=1), ("head", "key"))
     exp_logit = jnp.exp(logits - top_logit[:, None])
-    logit_sum = lax.psum(jnp.sum(exp_logit, axis=1), ("head", "key"))
+    logit_sum = jnp.sum(exp_logit, axis=1)
+    for mesh_axis in ("key", "head"):
+        logit_sum = lax.psum(logit_sum, mesh_axis)
     soft_probs = exp_logit / logit_sum[:, None]
     key_total = index_keys.shape[0] * head_count * key_count
     dlogits = key_total * (soft_probs - target)

time: 1500 us -> 1250 us (0.83)
  blocking collectives: 1410 us -> 1100 us
  waiting for transfers between devices: 0.05 us -> 57.4 us
    psum x1, blocking collectives: 342 us -> 35.9 us  [shards(): logit_sum = lax.psum(logit_sum, mesh_axis)]
    psum x1, waiting for transfers between devices: 0.01 us -> 57.3 us  [shards(): summed_all = lax.psum(spread, 'head')]
  transfers between devices with their start and end apart: 3 -> 3, of which waited for: 0 -> 1; matrix products, arithmetic and copies ran while one was open for 1% -> 1% of each run, Pallas kernels for 0% -> 0%
where the time goes in v1:
time: 1250 us
  blocking collectives  1100 us (88%)
  waiting for transfers between devices  57.4 us (5%)
  matrix products  32.4 us (3%)
  other arithmetic  22.8 us (2%)
  local copies, waits for them, and re-layouts  22.1 us (2%)
  between operations  13.9 us (1%)
    psum x1, blocking collectives, shards(): lax.psum((query_part, weight_part), ('head', 'key'))  688 us
    pmax x1, blocking collectives, shards(): top_logit = lax.pmax(jnp.max(logits, axis=1), ('head', 'key'))  347 us
    psum x1, waiting for transfers between devices, shards(): summed_all = lax.psum(spread, 'head')  57.3 us
    psum x1, blocking collectives, shards(): logit_sum = lax.psum(logit_sum, mesh_axis)  35.9 us
  transfers between devices with their start and end apart: 3, of which 1 were waited for; matrix products, arithmetic and copies ran while one was open for 1% of the time, Pallas kernels for 0%

profile of v1, /device:TPU:0, one launch (start us, length us, event | category | flops | bytes accessed | tf_op | source)
XLA Modules:
  0.0 1251.8 jit_solution(4740036782024080848)
XLA Ops:
  7.2 0.0 copy-start
  7.2 0.0 all-reduce.4.cloned.1.call-start
  7.2 7.2 copy.19
  14.4 8.3 reshape.73
  22.7 0.0 copy-done
  22.7 0.0 copy-start.1
  22.7 0.0 copy-start.3
  22.7 0.0 copy-start.4
  22.8 12.8 %multiply_reduce_fusion.1 = (f32[128,8]{0,1:T(8,128)S(1)}, f32[128,8,4096]{2,0,1:T(8,128)}) fusion(bf16[128,8,576]{0,2,1:T(8,128)(2,1)S(1)} %copy-done, bf16[4096,576,1]{0,1,2:T(8,128)(2,1)} %reshape.73), kind=kOutput, calls=%fused_computation.2 | convolution fusion | flops 4840225792 | bytes 22679552 | tf_op jit(solution)/shard_map/thd,sd->ths/dot_general | solution.py:17
  35.5 18.2 %pmax.15 = f32[128,8]{0,1:T(8,128)S(1)} all-reduce(f32[128,8]{0,1:T(8,128)S(1)} %get-tuple-element.14), channel_id=1, replica_groups=mesh['head'=16,'key'=8,'row'=2] {'key'}, use_global_device_ids=true, to_apply=%region_7.0 | all-reduce | flops 1024 | bytes 8192 | tf_op jit(solution)/shard_map/pmax | solution.py:20
  53.8 0.0 copy-done.1
  53.8 0.0 copy-done.3
  53.8 0.0 copy-done.4
  53.8 6.8 multiply_reduce_fusion.3
  60.6 0.1 multiply_reduce_fusion.4
  60.7 346.6 %pmax.14 = f32[128]{0:T(128)S(1)} all-reduce(f32[128]{0:T(128)S(1)} %multiply_reduce_fusion.4), channel_id=1, replica_groups=mesh['head'=16,'key'=8,'row'=2] {'head','key'}, use_global_device_ids=true, to_apply=%region_2.0 | all-reduce | flops 128 | bytes 1024 | tf_op jit(solution)/shard_map/pmax | solution.py:36
  407.3 0.2 exponential_reduce_fusion
  407.5 8.6 fusion
  416.1 14.6 %all-reduce = (f32[128,8]{0,1:T(8,128)S(1)}, f32[128]{0:T(128)S(1)}) all-reduce(f32[128,8]{0,1:T(8,128)S(1)} %fusion, f32[128]{0:T(128)S(1)} %exponential_reduce_fusion), channel_id=1, replica_groups=mesh['head'=16,'key'=8,'row'=2] {'key'}, use_global_device_ids=true, to_apply=%region_9.0 | all-reduce | flops 1152 | bytes 9216 | tf_op jit(solution)/shard_map/psum | solution.py:22
  430.7 8.0 multiply_reduce_fusion
  438.7 0.2 broadcast_multiply_fusion
  438.9 1.8 copy.20
  440.7 2.9 copy.21
  443.7 0.0 all-reduce.4.cloned.1.call-update
  443.7 0.0 all-reduce.6.cloned.1.call-start
  443.7 35.9 %psum.43 = f32[128]{0:T(128)S(1)} all-reduce(f32[128]{0:T(128)S(1)} %get-tuple-element.13), channel_id=1, replica_groups=mesh['head'=16,'key'=8,'row'=2] {'head'}, use_global_device_ids=true, to_apply=%region_5.0 | all-reduce | flops 128 | bytes 1024 | tf_op jit(solution)/shard_map/psum | solution.py:40
  479.6 57.3 %all-reduce.4.cloned.1.call-done = f32[128,16,256]{2,0,1:T(8,128)} async-done(((f32[128,16,256]{2,0,1:T(8,128)}), f32[128,16,256]{2,0,1:T(8,128)}) %all-reduce.4.cloned.1.call-update) | async-done | bytes 2097168 | tf_op jit(solution)/shard_map/psum | solution.py:26
  537.0 1.0 fusion.12
  538.0 5.8 fusion.13
  543.8 0.0 copy-start.2
  543.8 0.0 copy-start.5
  543.8 0.0 all-reduce.6.cloned.1.call-update
  543.8 0.0 reduce-scatter.2.cloned.1.call-start
  543.9 4.7 multiply_reduce_fusion.2
  548.5 0.0 copy-done.2
  548.6 0.0 copy-done.5
  548.6 7.0 fusion.5
  555.6 0.0 reduce-scatter.2.cloned.1.call-update
  555.6 687.8 %psum.47 = f32[128,64]{0,1:T(8,128)} all-reduce(f32[128,64]{0,1:T(8,128)S(1)} %broadcast_multiply_fusion.1), channel_id=1, replica_groups=mesh['head'=16,'key'=8,'row'=2] {'head','key'}, use_global_device_ids=true, to_apply=%region_15.16 | all-reduce | flops 8192 | bytes 65536 | tf_op jit(solution)/shard_map/psum | solution.py:59
  1243.5 0.0 all-reduce.6.cloned.1.call-done
  1243.5 1.0 constant_dynamic-slice_fusion
  1244.4 0.9 copy.24
  1245.3 0.0 reduce-scatter.2.cloned.1.call-done
  (2 shorter events, 0.0 us)
Async XLA Ops:
  7.2 15.6 %copy-start = (bf16[128,8,576]{0,2,1:T(8,128)(2,1)S(1)}, bf16[128,8,576]{0,2,1:T(8,128)(2,1)}, u32[]{:S(2)}) copy-start(bf16[128,8,576]{0,2,1:T(8,128)(2,1)} %param.5) | copy-start | bytes 3538948
  7.2 529.8 %all-reduce.4.cloned.1.call-start = ((), (), s32[]{:S(2)}) async-start(), calls=%async_computation.1 | async-start | bytes 4194304 | tf_op jit(solution)/shard_map/psum | solution.py:26
  22.7 31.0 %copy-start.1 = (bf16[128,64,128]{2,1,0:T(8,128)(2,1)S(1)}, bf16[128,64,128]{2,1,0:T(8,128)(2,1)}, u32[]{:S(2)}) copy-start(bf16[128,64,128]{2,1,0:T(8,128)(2,1)} %param.7) | copy-start | bytes 6291460
  22.7 31.0 %copy-start.3 = (bf16[256,128]{1,0:T(8,128)(2,1)S(1)}, bf16[256,128]{1,0:T(8,128)(2,1)}, u32[]{:S(2)}) copy-start(bf16[256,128]{1,0:T(8,128)(2,1)} %param.8) | copy-start | bytes 196612
  22.7 31.0 %copy-start.4 = (f32[128,64]{0,1:T(8,128)S(1)}, f32[128,64]{0,1:T(8,128)}, u32[]{:S(2)}) copy-start(f32[128,64]{0,1:T(8,128)} %param.9) | copy-start | bytes 98308
  443.7 799.8 %all-reduce.6.cloned.1.call-start = ((), (), s32[]{:S(2)}) async-start(), calls=%async_computation.2 | async-start | bytes 8388608 | tf_op jit(solution)/shard_map/psum | solution.py:59
  543.8 4.8 copy-start.2
  543.8 4.8 copy-start.5
  543.8 701.5 %reduce-scatter.2.cloned.1.call-start = ((), (), s32[]{:S(2)}) async-start(), calls=%async_computation.3 | async-start | bytes 196608 | tf_op jit(solution)/shard_map/reduce_scatter | solution.py:57
Sparse Core Ops, SparseCore 0:
  443.8 93.1 all-reduce.3
  543.9 234.7 all-reduce.5
  781.8 9.8 reduce-scatter.1

commit v2 on v0

--- a/solution.py
+++ b/solution.py
@@ -5,6 +5,11 @@
 from jax.sharding import PartitionSpec as P
 
 MH = 128
+
+
+def by_each_axis(array, one, other):
+    inner = lax.psum(array, one)
+    return lax.psum(inner, other)
 
 
 def shards(mla_query, mla_cache, index_query, index_keys, index_weight):
@@ -54,7 +59,7 @@
     )
     key_grad = lax.psum_scatter(keys_part, "row", scatter_dimension=0, tiled=True)
     head_share = query_part.shape[1] // head_count
-    query_full, weight_grad = lax.psum((query_part, weight_part), ("head", "key"))
+    query_full, weight_grad = by_each_axis((query_part, weight_part), "head", "key")
     query_grad = lax.dynamic_slice_in_dim(
         query_full, lax.axis_index("head") * head_share, head_share, 1
     )

time: 1500 us -> 1040 us (0.69)
  blocking collectives: 1410 us -> 827 us
  waiting for transfers between devices: 0.05 us -> 116 us
    psum x1 -> x2, blocking collectives: 684 us -> 103 us  [the longest x1 72.4 us: by_each_axis(): inner = lax.psum(array, one)]
    psum x1 -> x2, waiting for transfers between devices: 0.01 us -> 106 us  [the longest x1 106 us: by_each_axis(): inner = lax.psum(array, one)]
  transfers between devices with their start and end apart: 3 -> 4, of which waited for: 0 -> 2; matrix products, arithmetic and copies ran while one was open for 1% -> 2% of each run, Pallas kernels for 0% -> 0%
where the time goes in v2:
time: 1040 us; the launch traced here: 1030 us
  blocking collectives  827 us (80%)
  waiting for transfers between devices  116 us (11%)
  matrix products  32.1 us (3%)
  other arithmetic  22.6 us (2%)
  local copies, waits for them, and re-layouts  22.2 us (2%)
  between operations  13.9 us (1%)
    pmax x1, blocking collectives, shards(): top_logit = lax.pmax(jnp.max(logits, axis=1), ('head', 'key'))  349 us
    psum x1, blocking collectives, shards(): logit_sum = lax.psum(jnp.sum(exp_logit, axis=1), ('head', 'key'))  342 us
    psum x1, waiting for transfers between devices, by_each_axis(): inner = lax.psum(array, one)  106 us
    psum x1, blocking collectives, by_each_axis(): inner = lax.psum(array, one)  72.4 us
    psum x1, blocking collectives, by_each_axis(): return lax.psum(inner, other)  31 us
  transfers between devices with their start and end apart: 4, of which 2 were waited for; matrix products, arithmetic and copies ran while one was open for 2% of the time, Pallas kernels for 0%

profile of v2, /device:TPU:0, one launch (start us, length us, event | category | flops | bytes accessed | tf_op | source)
XLA Modules:
  0.0 1034.1 jit_solution(6784016708318351702)
XLA Ops:
  7.2 0.0 copy-start
  7.2 0.0 all-reduce.4.cloned.1.call-start
  7.2 7.2 copy.19
  14.4 8.3 reshape.73
  22.7 0.0 copy-done
  22.7 12.6 %multiply_reduce_fusion.1 = (f32[128,8]{0,1:T(8,128)S(1)}, f32[128,8,4096]{2,0,1:T(8,128)}) fusion(bf16[128,8,576]{0,2,1:T(8,128)(2,1)S(1)} %copy-done, bf16[4096,576,1]{0,1,2:T(8,128)(2,1)} %reshape.73), kind=kOutput, calls=%fused_computation.2 | convolution fusion | flops 4840225792 | bytes 22679552 | tf_op jit(solution)/shard_map/thd,sd->ths/dot_general | solution.py:22
  35.3 18.2 %pmax.15 = f32[128,8]{0,1:T(8,128)S(1)} all-reduce(f32[128,8]{0,1:T(8,128)S(1)} %get-tuple-element.12), channel_id=1, replica_groups=mesh['head'=16,'key'=8,'row'=2] {'key'}, use_global_device_ids=true, to_apply=%region_6.0 | all-reduce | flops 1024 | bytes 8192 | tf_op jit(solution)/shard_map/pmax | solution.py:25
  53.6 8.6 fusion
  62.2 14.2 %psum.50 = f32[128,8]{0,1:T(8,128)S(1)} all-reduce(f32[128,8]{0,1:T(8,128)S(1)} %fusion), channel_id=1, replica_groups=mesh['head'=16,'key'=8,'row'=2] {'key'}, use_global_device_ids=true, to_apply=%region_8.0 | all-reduce | flops 1024 | bytes 8192 | tf_op jit(solution)/shard_map/psum | solution.py:27
  76.4 8.0 multiply_reduce_fusion
  84.4 0.0 copy-start.2
  84.4 0.0 copy-start.3
  84.4 0.2 broadcast_multiply_fusion
  84.6 1.9 copy.20
  86.4 3.0 copy.21
  89.4 0.0 all-reduce.4.cloned.1.call-update
  89.4 0.2 all-reduce.6.cloned.1.call-start
  89.7 0.0 copy-done.2
  89.7 0.0 copy-done.3
  89.7 6.8 multiply_reduce_fusion.3
  96.4 0.1 multiply_reduce_fusion.4
  96.5 349.1 %pmax.14 = f32[128]{0:T(128)S(1)} all-reduce(f32[128]{0:T(128)S(1)} %multiply_reduce_fusion.4), channel_id=1, replica_groups=mesh['head'=16,'key'=8,'row'=2] {'head','key'}, use_global_device_ids=true, to_apply=%region_2.0 | all-reduce | flops 128 | bytes 1024 | tf_op jit(solution)/shard_map/pmax | solution.py:41
  445.7 0.2 exponential_reduce_fusion
  445.9 342.2 %psum.49 = f32[128]{0:T(128)S(1)} all-reduce(f32[128]{0:T(128)S(1)} %exponential_reduce_fusion), channel_id=1, replica_groups=mesh['head'=16,'key'=8,'row'=2] {'head','key'}, use_global_device_ids=true, to_apply=%region_4.0 | all-reduce | flops 128 | bytes 1024 | tf_op jit(solution)/shard_map/psum | solution.py:43
  788.0 0.0 all-reduce.4.cloned.1.call-done
  788.0 1.0 fusion.12
  789.1 5.7 fusion.13
  794.8 0.0 copy-start.1
  794.8 0.0 all-reduce.6.cloned.1.call-update
  794.8 0.0 all-reduce.8.cloned.1.call-start
  794.9 106.4 %all-reduce.6.cloned.1.call-done = f32[128,64,128]{2,0,1:T(8,128)} async-done(((f32[128,64,128]{2,0,1:T(8,128)}), f32[128,64,128]{2,0,1:T(8,128)}) %all-reduce.6.cloned.1.call-update) | async-done | bytes 4194320 | tf_op jit(solution)/shard_map/psum | solution.py:11
  901.3 0.0 all-reduce.8.cloned.1.call-update
  901.3 0.0 reduce-scatter.2.cloned.1.call-start
  901.3 4.5 multiply_reduce_fusion.2
  905.9 0.0 copy-done.1
  905.9 7.0 fusion.5
  912.9 0.0 reduce-scatter.2.cloned.1.call-update
  913.0 72.4 %psum.54 = f32[128,64]{0,1:T(8,128)S(1)} all-reduce(f32[128,64]{0,1:T(8,128)S(1)} %broadcast_multiply_fusion.1), channel_id=1, replica_groups=mesh['head'=16,'key'=8,'row'=2] {'head'}, use_global_device_ids=true, to_apply=%region_15.16 | all-reduce | flops 8192 | bytes 65536 | tf_op jit(solution)/shard_map/psum | solution.py:11
  985.3 31.0 %psum.55 = f32[128,64]{0,1:T(8,128)} all-reduce(f32[128,64]{0,1:T(8,128)S(1)} %psum.54), channel_id=1, replica_groups=mesh['head'=16,'key'=8,'row'=2] {'key'}, use_global_device_ids=true, to_apply=%region_16.17 | all-reduce | flops 8192 | bytes 65536 | tf_op jit(solution)/shard_map/psum | solution.py:12
  1016.3 0.0 all-reduce.8.cloned.1.call-done
  1016.3 1.0 constant_dynamic-slice_fusion
  1017.3 0.9 copy.24
  1018.1 9.5 reduce-scatter.2.cloned.1.call-done
  (2 shorter events, 0.0 us)
Async XLA Ops:
  7.2 15.6 %copy-start = (bf16[128,8,576]{0,2,1:T(8,128)(2,1)S(1)}, bf16[128,8,576]{0,2,1:T(8,128)(2,1)}, u32[]{:S(2)}) copy-start(bf16[128,8,576]{0,2,1:T(8,128)(2,1)} %param.5) | copy-start | bytes 3538948
  7.2 780.8 %all-reduce.4.cloned.1.call-start = ((), (), s32[]{:S(2)}) async-start(), calls=%async_computation.1 | async-start | bytes 4194304 | tf_op jit(solution)/shard_map/psum | solution.py:31
  84.4 5.3 copy-start.2
  84.4 5.3 copy-start.3
  89.4 811.8 %all-reduce.6.cloned.1.call-start = ((), (), s32[]{:S(2)}) async-start(), calls=%async_computation.2 | async-start | bytes 8388608 | tf_op jit(solution)/shard_map/psum | solution.py:11
  794.8 111.1 %copy-start.1 = (bf16[128,64,128]{2,1,0:T(8,128)(2,1)S(1)}, bf16[128,64,128]{2,1,0:T(8,128)(2,1)}, u32[]{:S(2)}) copy-start(bf16[128,64,128]{2,1,0:T(8,128)(2,1)} %param.7) | copy-start | bytes 6291460
  794.8 221.5 %all-reduce.8.cloned.1.call-start = ((), (), s32[]{:S(2)}) async-start(), calls=%async_computation.3 | async-start | bytes 8388608 | tf_op jit(solution)/shard_map/psum | solution.py:12
  901.3 126.3 %reduce-scatter.2.cloned.1.call-start = ((), (), s32[]{:S(2)}) async-start(), calls=%async_computation.4 | async-start | bytes 196608 | tf_op jit(solution)/shard_map/reduce_scatter | solution.py:60
Sparse Core Ops, SparseCore 0:
  89.5 99.6 all-reduce.3
  795.0 106.2 all-reduce.5
  903.8 109.4 all-reduce.7
  1016.3 11.2 reduce-scatter.1
